TPU v7x, 32 devices: a whole 2x2x4 slice. The times are simulated.
32 devices in a mesh: groups: 2 (over x), chan: 16 (over z, y, core).
Axes of the slice: x: 2, y: 2, z: 4, core: 2. Of those that a mesh axis runs over, the one named last changes fastest.
Arguments:
- raw: bfloat16 [5120, 4096], P('chan', 'groups'), parts along dimension 1, may hold values from -50 to 50
- taps: bfloat16 [255], replicated, may hold values from -0.375 to 0.375
- tile_dist: int32 [16, 8], P('chan', 'groups'), parts along dimension 1, may hold values from 1 to 4, as said below
- tile_count: int32 [32], P(('groups', 'chan')), parts along dimension 0, may hold values from 0 to 4
- owner: int32 [8], P('groups'), parts along dimension 0, may hold values from 0 to 15, as said below
Outputs:
- band_stack: float32 [16, 256, 128], P('chan', 'groups'), parts along dimension 1
There are 2 independent parts, one for each index of `groups`. A program takes and returns all parts, laid end to end along the dimension named above; an argument that names none is the same for every part. Nothing has to cross between parts.
Inputs may be any that keep to these rules, and one draw needn't show every extreme that they name: Each row of tile_dist holds every distance of 1 to 4 once; in row i the first tile_count[i] entries d satisfy i + d < 16. `owner`: the owners are distinct, and some band is owned by index 15.
All inputs are finite; a program needn't handle non-finite values.
Results may differ from a plain program's by a relative error of at most 0.014.
Values may be sent and summed in bfloat16 or wider, within the bound.
A program may use at most 128 MiB of HBM per device.

v0:
```python
import math
import jax
import jax.numpy as jnp
from jax import lax
from jax.sharding import PartitionSpec as P


def extended(x, sides, width):
    for axis, dim in sides:
        size, length = (lax.axis_size(axis), x.shape[dim])
        up = [(i, (i + 1) % size) for i in range(size - 1)]
        down = [(j, i) for i, j in up]
        last = lax.slice_in_dim(x, length - width, length, axis=dim)
        initial = lax.slice_in_dim(x, 0, width, axis=dim)
        before = lax.ppermute(last, axis, up)
        after = lax.ppermute(initial, axis, down)
        x = jnp.concatenate([before, x, after], axis=dim)
    return x


def passed_along(x, axis, by):
    size = lax.axis_size(axis)
    pairs = [(i, i + by) for i in range(size) if 0 <= i + by < size]
    return lax.ppermute(x, axis, pairs)


def band_matrix(taps, out_rows, in_cols):
    width = taps.shape[0]
    offset = (
        jnp.arange(in_cols, dtype=jnp.int32)[None, :]
        - 5 * jnp.arange(out_rows, dtype=jnp.int32)[:, None]
    )
    inside = (offset >= 0) & (offset < width)
    picked = jnp.take(taps, jnp.clip(offset, 0, width - 1))
    return jnp.where(inside, picked, jnp.zeros_like(picked))


def whiten(block):
    length, channels = block.shape
    bins = length // 16
    freqs = jnp.arange(1, bins + 1, dtype=jnp.int32)[:, None]
    times = jnp.arange(length, dtype=jnp.int32)[None, :]
    angle = (freqs * times % length).astype(jnp.float32) * (2.0 * math.pi / length)
    table = jnp.concatenate([jnp.cos(angle), -jnp.sin(angle)], axis=0)
    table_high = table.astype(jnp.bfloat16)
    table_low = (table - table_high.astype(jnp.float32)).astype(jnp.bfloat16)
    spectrum = jnp.dot(table_high, block, preferred_element_type=jnp.float32)
    spectrum = spectrum + jnp.dot(table_low, block, preferred_element_type=jnp.float32)
    squares = spectrum * spectrum
    power = jnp.sum(squares[:bins] + squares[bins:], axis=1) / (2 * channels)
    gain = lax.rsqrt(power + 1e-06)
    return (spectrum * jnp.concatenate([gain, gain])[:, None]).astype(jnp.bfloat16)


def cross_tile(mine, partner, scale):
    product = lax.dot_general(
        mine, partner, (((0,), (0,)), ((), ())), preferred_element_type=jnp.float32
    )
    return product * scale


def shards(raw, taps, tile_dist, tile_count, owner):
    rows = raw.shape[0]
    width = taps.shape[0]
    half = (width - 1) // 2
    out_rows = rows // 5
    banded = band_matrix(taps, out_rows, rows + 2 * half)
    padded = extended(raw, (("chan", 0),), half)
    filtered = jnp.dot(banded, padded, preferred_element_type=jnp.float32)
    decimated = filtered.astype(jnp.bfloat16)
    regrouped = lax.all_to_all(decimated, "chan", split_axis=1, concat_axis=0, tiled=True)
    whitened = whiten(regrouped)
    channels = whitened.shape[1]
    scale = 1.0 / whitened.shape[0]
    bands = tile_dist.shape[1]
    slots = jnp.arange(bands, dtype=jnp.int32) < tile_count[0]
    partner = whitened
    stacks = []
    for distance in range(1, bands + 1):
        partner = passed_along(whitened, "chan", -distance)
        listed = jnp.sum(((tile_dist[0] == distance) & slots).astype(jnp.int32))
        tile = lax.cond(
            listed > 0,
            lambda first, second: cross_tile(first, second, scale),
            lambda first, second: jnp.zeros((channels, channels), jnp.float32),
            whitened,
            partner,
        )
        stacks.append(tile)
    stacked = jnp.stack(stacks)
    totals = lax.psum(stacked, "chan")
    selected = (owner == lax.axis_index("chan")).astype(jnp.float32)
    return jnp.einsum("b,bxy->xy", selected, totals, precision=lax.Precision.HIGHEST)[None]


def solution(mesh):
    in_specs = (P("chan", "groups"), P(), P("chan", "groups"), P(("groups", "chan")), P("groups"))
    out_specs = P("chan", "groups", None)
    return jax.shard_map(shards, mesh=mesh, in_specs=in_specs, out_specs=out_specs, check_vma=False)
```

profile of v0, /device:TPU:1, one launch (start us, length us, event | category | flops | bytes accessed | tf_op | source)
XLA Modules:
  0.0 350.2 jit_solution(16321516343890510298)
XLA Ops:
  6.5 1.3 fusion.63
  7.9 4.5 %collective-permute-start = (bf16[127,2048]{1,0:T(8,128)(2,1)S(1)}, bf16[127,2048]{1,0:T(8,128)(2,1)S(1)}, u32[]{:S(2)}, u32[]{:S(2)}) collective-permute-start(bf16[127,2048]{1,0:T(8,128)(2,1)S(1)} %get-tuple-element.49), channel_id=1, source_target_pairs={{0,1},{1,2},{2,3},{3,4},{4,5},{5,6},{6,7},{7,8},{8,9},{9,10},{10,1... | collective-permute-start | bytes 1560584 | tf_op jit(solution)/shard_map/ppermute | solution.py:15
  12.4 1.9 collective-permute-start.1
  14.4 0.1 compare_select_fusion
  14.5 0.2 reshape.83
  14.7 202.9 %gather_fusion = bf16[36736]{0:T(1024)(128)(2,1)S(1)} fusion(bf16[255]{0:T(256)(128)(2,1)S(1)} %copy-done, s32[36864]{0:T(1024)S(1)} %pad_clamp_fusion), kind=kCustom, calls=%fused_computation | custom fusion | bytes 293888 | tf_op jit(solution)/shard_map/jit(_take)/gather | solution.py:34
  217.7 0.2 reshape.82
  217.9 1.9 fusion.13
  219.8 0.8 copy.13
  220.6 6.5 %all-to-all-start = ((bf16[64,16,128]{2,0,1:T(8,128)(2,1)}), bf16[64,16,128]{2,0,1:T(8,128)(2,1)S(1)}, u32[]{:S(2)}, u32[]{:S(2)}) async-start(bf16[64,16,128]{2,0,1:T(8,128)(2,1)} %bitcast.58), calls=%async_computation | async-start | bytes 524288 | tf_op jit(solution)/shard_map/all_to_all | solution.py:71
  227.1 0.0 all-reduce.2.cloned.1.call-start
  227.8 1.1 fusion.35
  228.9 7.7 %all-to-all-done = bf16[64,16,128]{2,0,1:T(8,128)(2,1)S(1)} async-done(((bf16[64,16,128]{2,0,1:T(8,128)(2,1)}), bf16[64,16,128]{2,0,1:T(8,128)(2,1)S(1)}, u32[]{:S(2)}, u32[]{:S(2)}) %all-to-all-start) | async-done | bytes 262176 | tf_op jit(solution)/shard_map/all_to_all | solution.py:71
  236.5 0.2 fusion.17
  236.8 0.2 fusion.64
  237.0 0.1 fusion.43
  237.1 0.1 pad_maximum_fusion.2
  237.2 0.1 multiply_convert_fusion
  237.3 2.6 collective-permute-start.2
  239.9 1.3 collective-permute-start.3
  241.2 1.3 collective-permute-start.4
  242.5 1.3 collective-permute-start.5
  243.8 0.7 fusion.50
  247.1 0.2 conditional.5
  247.1 0.2 fusion.1
  247.3 0.5 collective-permute-done.4
  247.8 1.3 collective-permute-done.5
  249.2 0.2 conditional.7
  249.2 0.2 fusion.3
  249.4 0.7 pad_maximum_fusion.1
  250.1 91.1 %all-reduce.2.cloned.1.call-done = f32[4,128,128]{2,1,0:T(8,128)} async-done(((f32[4,128,128]{2,1,0:T(8,128)}), f32[4,128,128]{2,1,0:T(8,128)}) %all-reduce.2.cloned.1.call-update) | async-done | bytes 262160 | tf_op jit(solution)/shard_map/psum | solution.py:91
  341.3 2.1 fusion.22
  (21 shorter events, 0.1 us)
Async XLA Ops:
  6.5 8.2 %copy-start = (bf16[255]{0:T(256)(128)(2,1)S(1)}, bf16[255]{0:T(256)(128)(2,1)}, u32[]{:S(2)}) copy-start(bf16[255]{0:T(256)(128)(2,1)} %param.14) | copy-start | bytes 1534
  7.9 210.0 %collective-permute-start = (bf16[127,2048]{1,0:T(8,128)(2,1)S(1)}, bf16[127,2048]{1,0:T(8,128)(2,1)S(1)}, u32[]{:S(2)}, u32[]{:S(2)}) collective-permute-start(bf16[127,2048]{1,0:T(8,128)(2,1)S(1)} %get-tuple-element.49), channel_id=1, source_target_pairs={{0,1},{1,2},{2,3},{3,4},{4,5},{5,6},{6,7},{7,8},{8,9},{9,10},{10,1... | collective-permute-start | bytes 1560584 | tf_op jit(solution)/shard_map/ppermute | solution.py:15
  12.4 205.5 %collective-permute-start.1 = (bf16[127,2048]{1,0:T(8,128)(2,1)S(1)}, bf16[127,2048]{1,0:T(8,128)(2,1)}, u32[]{:S(2)}, u32[]{:S(2)}) collective-permute-start(bf16[127,2048]{1,0:T(8,128)(2,1)S(1)} %get-tuple-element.50), channel_id=1, source_target_pairs={{1,0},{2,1},{3,2},{4,3},{5,4},{6,5},{7,6},{8,7},{9,8},{10,9},{11,1... | collective-permute-start | bytes 1560584 | tf_op jit(solution)/shard_map/ppermute | solution.py:16
  14.7 203.2 %copy-start.1 = (bf16[320,2048]{1,0:T(8,128)(2,1)S(1)}, bf16[320,2048]{1,0:T(8,128)(2,1)}, u32[]{:S(2)}) copy-start(bf16[320,2048]{1,0:T(8,128)(2,1)} %param.13) | copy-start | bytes 3932164
  220.6 15.9 %all-to-all-start = ((bf16[64,16,128]{2,0,1:T(8,128)(2,1)}), bf16[64,16,128]{2,0,1:T(8,128)(2,1)S(1)}, u32[]{:S(2)}, u32[]{:S(2)}) async-start(bf16[64,16,128]{2,0,1:T(8,128)(2,1)} %bitcast.58), calls=%async_computation | async-start | bytes 524288 | tf_op jit(solution)/shard_map/all_to_all | solution.py:71
  227.0 16.7 %copy-start.3 = (s32[1,4]{1,0:T(1,128)S(1)}, s32[1,4]{1,0:T(1,128)}, u32[]{:S(2)}) copy-start(s32[1,4]{1,0:T(1,128)} %param.15) | copy-start | bytes 52
  227.1 114.2 %all-reduce.2.cloned.1.call-start = ((), (), s32[]{:S(2)}) async-start(), calls=%async_computation.1 | async-start | bytes 524288 | tf_op jit(solution)/shard_map/psum | solution.py:91
  236.8 104.5 %copy-start.2 = (s32[4]{0:T(128)S(1)}, s32[4]{0:T(128)}, u32[]{:S(2)}) copy-start(s32[4]{0:T(128)} %param.17) | copy-start | bytes 52
  237.3 9.7 %collective-permute-start.2 = (bf16[128,128]{1,0:T(8,128)(2,1)S(1)}, bf16[128,128]{1,0:T(8,128)(2,1)S(1)}, u32[]{:S(2)}, u32[]{:S(2)}) collective-permute-start(bf16[128,128]{1,0:T(8,128)(2,1)S(1)} %multiply_convert_fusion), channel_id=1, source_target_pairs={{1,0},{2,1},{3,2},{4,3},{5,4},{6,5},{7,6},{8,7},{9,8},{10,9},{11,1... | collective-permute-start | bytes 98312 | tf_op jit(solution)/shard_map/ppermute | solution.py:24
  239.9 7.2 %collective-permute-start.3 = (bf16[128,128]{1,0:T(8,128)(2,1)S(1)}, bf16[128,128]{1,0:T(8,128)(2,1)S(1)}, u32[]{:S(2)}, u32[]{:S(2)}) collective-permute-start(bf16[128,128]{1,0:T(8,128)(2,1)S(1)} %multiply_convert_fusion), channel_id=1, source_target_pairs={{2,0},{3,1},{4,2},{5,3},{6,4},{7,5},{8,6},{9,7},{10,8},{11,9},{12,... | collective-permute-start | bytes 98312 | tf_op jit(solution)/shard_map/ppermute | solution.py:24
  241.2 6.7 %collective-permute-start.4 = (bf16[128,128]{1,0:T(8,128)(2,1)S(1)}, bf16[128,128]{1,0:T(8,128)(2,1)S(1)}, u32[]{:S(2)}, u32[]{:S(2)}) collective-permute-start(bf16[128,128]{1,0:T(8,128)(2,1)S(1)} %multiply_convert_fusion), channel_id=1, source_target_pairs={{3,0},{4,1},{5,2},{6,3},{7,4},{8,5},{9,6},{10,7},{11,8},{12,9},{13... | collective-permute-start | bytes 98312 | tf_op jit(solution)/shard_map/ppermute | solution.py:24
  242.5 6.7 %collective-permute-start.5 = (bf16[128,128]{1,0:T(8,128)(2,1)S(1)}, bf16[128,128]{1,0:T(8,128)(2,1)S(1)}, u32[]{:S(2)}, u32[]{:S(2)}) collective-permute-start(bf16[128,128]{1,0:T(8,128)(2,1)S(1)} %multiply_convert_fusion), channel_id=1, source_target_pairs={{4,0},{5,1},{6,2},{7,3},{8,4},{9,5},{10,6},{11,7},{12,8},{13,9},{1... | collective-permute-start | bytes 98312 | tf_op jit(solution)/shard_map/ppermute | solution.py:24
Sparse Core Ops, SparseCore 0:
  250.2 90.9 all-reduce.1
where the time goes:
time: 351 us; the launch traced here: 350 us
  local copies, waits for them, and re-layouts  205 us (58%)
  waiting for transfers between devices  101 us (29%)
  starting transfers between devices  19.4 us (6%)
  between operations  16.8 us (5%)
  matrix products  4.78 us (1%)
    gather x2, local copies, waits for them, and re-layouts, band_matrix(): picked = jnp.take(taps, jnp.clip(offset, 0, width - 1))  203 us
    psum x1, waiting for transfers between devices, shards(): totals = lax.psum(stacked, 'chan')  91.1 us
    all_to_all x1, waiting for transfers between devices, shards(): lax.all_to_all(decimated, 'chan', split_axis=1, concat_axis=0, tiled=True)  7.67 us
  transfers between devices with their start and end apart: 8, of which 4 were waited for; matrix products, arithmetic and copies ran while one was open for 59% of the time, Pallas kernels for 0%

commit v1 on v0

--- a/solution.py
+++ b/solution.py
@@ -3,6 +3,18 @@
 import jax.numpy as jnp
 from jax import lax
 from jax.sharding import PartitionSpec as P
+
+
+def split_up(shard, dim, size):
+    dims = shard.shape
+    tiles = shard.reshape(*dims[:dim], size, dims[dim] // size, *dims[dim + 1 :])
+    return jnp.moveaxis(tiles, dim, 0)
+
+
+def joined_along(blocks, dim):
+    shape = list(blocks.shape[1:])
+    shape[dim] *= blocks.shape[0]
+    return jnp.moveaxis(blocks, 0, dim).reshape(shape)
 
 
 def extended(x, sides, width):
@@ -68,7 +80,14 @@
     padded = extended(raw, (("chan", 0),), half)
     filtered = jnp.dot(banded, padded, preferred_element_type=jnp.float32)
     decimated = filtered.astype(jnp.bfloat16)
-    regrouped = lax.all_to_all(decimated, "chan", split_axis=1, concat_axis=0, tiled=True)
+    size_2, here = (lax.axis_size("chan"), lax.axis_index("chan"))
+    blocks = split_up(decimated, 1, size_2)
+    gathered = [blocks[here]]
+    for turn in range(1, size_2):
+        sent = blocks[here ^ turn]
+        gathered.append(lax.ppermute(sent, "chan", [(i_2, i_2 ^ turn) for i_2 in range(size_2)]))
+    blocks = jnp.stack(gathered)[here ^ jnp.arange(size_2)]
+    regrouped = joined_along(blocks, 0)
     whitened = whiten(regrouped)
     channels = whitened.shape[1]
     scale = 1.0 / whitened.shape[0]

time: 351 us -> 364 us (1.037)
  starting transfers between devices: 19.4 us -> 34.3 us
    ppermute x0 -> x15, starting transfers between devices: none -> 21.6 us  [shards(): lax.ppermute(sent, 'chan', [(i_2, i_2 ^ turn) for i_2 in range(size_2)])]
    all_to_all x1 -> x0, waiting for transfers between devices: 7.67 us -> none  [shards(): lax.all_to_all(decimated, 'chan', split_axis=1, concat_axis=0, tiled=True)]
    all_to_all x1 -> x0, starting transfers between devices: 6.45 us -> none  [shards(): lax.all_to_all(decimated, 'chan', split_axis=1, concat_axis=0, tiled=True)]
    ppermute x0 -> x15, waiting for transfers between devices: none -> 4.6 us  [shards(): lax.ppermute(sent, 'chan', [(i_2, i_2 ^ turn) for i_2 in range(size_2)])]
  transfers between devices with their start and end apart: 8 -> 22, of which waited for: 4 -> 4; matrix products, arithmetic and copies ran while one was open for 59% -> 57% of each run, Pallas kernels for 0% -> 0%
where the time goes in v1:
time: 364 us
  local copies, waits for them, and re-layouts  206 us (57%)
  waiting for transfers between devices  98.2 us (27%)
  starting transfers between devices  34.3 us (9%)
  between operations  17.1 us (5%)
  matrix products  4.78 us (1%)
    gather x2, local copies, waits for them, and re-layouts, band_matrix(): picked = jnp.take(taps, jnp.clip(offset, 0, width - 1))  203 us
    psum x1, waiting for transfers between devices, shards(): totals = lax.psum(stacked, 'chan')  93.5 us
    ppermute x15, starting transfers between devices, shards(): lax.ppermute(sent, 'chan', [(i_2, i_2 ^ turn) for i_2 in range(size_2)])  21.6 us
  transfers between devices with their start and end apart: 22, of which 4 were waited for; matrix products, arithmetic and copies ran while one was open for 57% of the time, Pallas kernels for 0%

profile of v1, /device:TPU:1, one launch (start us, length us, event | category | flops | bytes accessed | tf_op | source)
XLA Modules:
  0.0 363.8 jit_solution(743818498014967686)
XLA Ops:
  6.5 1.3 fusion.64
  7.9 2.0 collective-permute-start.1
  9.9 4.5 %collective-permute-start = (bf16[127,2048]{1,0:T(8,128)(2,1)S(1)}, bf16[127,2048]{1,0:T(8,128)(2,1)}, u32[]{:S(2)}, u32[]{:S(2)}) collective-permute-start(bf16[127,2048]{1,0:T(8,128)(2,1)S(1)} %get-tuple-element.49), channel_id=1, source_target_pairs={{0,1},{1,2},{2,3},{3,4},{4,5},{5,6},{6,7},{7,8},{8,9},{9,10},{10,1... | collective-permute-start | bytes 1560584 | tf_op jit(solution)/shard_map/ppermute | solution.py:27
  15.5 202.9 %gather_fusion = bf16[36736]{0:T(1024)(128)(2,1)S(1)} fusion(bf16[255]{0:T(256)(128)(2,1)S(1)} %copy-done, s32[36864]{0:T(1024)S(1)} %pad_clamp_fusion), kind=kCustom, calls=%fused_computation | custom fusion | bytes 293888 | tf_op jit(solution)/shard_map/jit(_take)/gather | solution.py:46
  218.7 1.1 fusion.35
  219.9 1.9 fusion.13
  221.8 0.8 constant_dynamic-slice_fusion
  222.7 2.1 collective-permute-start.3
  224.9 0.5 collective-permute-start.4
  225.3 1.3 collective-permute-start.5
  226.6 0.7 collective-permute-start.6
  227.5 2.1 collective-permute-start.7
  229.6 0.5 collective-permute-start.8
  230.1 2.2 collective-permute-start.9
  232.3 0.7 collective-permute-start.10
  233.0 2.9 collective-permute-start.11
  236.0 0.6 collective-permute-start.12
  236.5 2.6 collective-permute-start.13
  239.1 1.2 collective-permute-start.14
  240.3 2.6 collective-permute-start.15
  242.9 1.6 collective-permute-start.16
  244.6 1.1 collective-permute-done.15
  245.7 3.5 collective-permute-done.16
  249.2 0.6 gather_fusion.1
  250.6 1.3 collective-permute-start.20
  251.9 1.3 collective-permute-start.19
  253.2 1.3 collective-permute-start.18
  254.5 2.4 collective-permute-start.17
  256.8 0.8 fusion.51
  260.7 0.7 pad_maximum_fusion.1
  261.4 93.5 %all-reduce.2.cloned.1.call-done = f32[4,128,128]{2,1,0:T(8,128)} async-done(((f32[4,128,128]{2,1,0:T(8,128)}), f32[4,128,128]{2,1,0:T(8,128)}) %all-reduce.2.cloned.1.call-update) | async-done | bytes 262160 | tf_op jit(solution)/shard_map/psum | solution.py:110
  354.9 2.1 fusion.21
  (84 shorter events, 2.6 us)
Async XLA Ops:
  6.5 8.9 %copy-start = (bf16[255]{0:T(256)(128)(2,1)S(1)}, bf16[255]{0:T(256)(128)(2,1)}, u32[]{:S(2)}) copy-start(bf16[255]{0:T(256)(128)(2,1)} %param.14) | copy-start | bytes 1534
  6.5 348.3 %all-reduce.2.cloned.1.call-start = ((), (), s32[]{:S(2)}) async-start(), calls=%async_computation | async-start | bytes 524288 | tf_op jit(solution)/shard_map/psum | solution.py:110
  7.9 211.9 %collective-permute-start.1 = (bf16[127,2048]{1,0:T(8,128)(2,1)S(1)}, bf16[127,2048]{1,0:T(8,128)(2,1)S(1)}, u32[]{:S(2)}, u32[]{:S(2)}) collective-permute-start(bf16[127,2048]{1,0:T(8,128)(2,1)S(1)} %get-tuple-element.50), channel_id=1, source_target_pairs={{1,0},{2,1},{3,2},{4,3},{5,4},{6,5},{7,6},{8,7},{9,8},{10,9},{11,1... | collective-permute-start | bytes 1560584 | tf_op jit(solution)/shard_map/ppermute | solution.py:28
  9.9 210.0 %collective-permute-start = (bf16[127,2048]{1,0:T(8,128)(2,1)S(1)}, bf16[127,2048]{1,0:T(8,128)(2,1)}, u32[]{:S(2)}, u32[]{:S(2)}) collective-permute-start(bf16[127,2048]{1,0:T(8,128)(2,1)S(1)} %get-tuple-element.49), channel_id=1, source_target_pairs={{0,1},{1,2},{2,3},{3,4},{4,5},{5,6},{6,7},{7,8},{8,9},{9,10},{10,1... | collective-permute-start | bytes 1560584 | tf_op jit(solution)/shard_map/ppermute | solution.py:27
  15.4 204.4 %copy-start.1 = (bf16[320,2048]{1,0:T(8,128)(2,1)S(1)}, bf16[320,2048]{1,0:T(8,128)(2,1)}, u32[]{:S(2)}) copy-start(bf16[320,2048]{1,0:T(8,128)(2,1)} %param.13) | copy-start | bytes 3932164
  222.6 4.9 %collective-permute-start.2 = (bf16[64,128]{1,0:T(8,128)(2,1)S(1)}, bf16[64,128]{1,0:T(8,128)(2,1)S(1)}, u32[]{:S(2)}, u32[]{:S(2)}) collective-permute-start(bf16[64,128]{1,0:T(8,128)(2,1)S(1)} %bitcast.154), channel_id=1, source_target_pairs={{0,1},{1,0},{2,3},{3,2},{4,5},{5,4},{6,7},{7,6},{8,9},{9,8},{10,11... | collective-permute-start | bytes 49160 | tf_op jit(solution)/shard_map/ppermute | solution.py:88
  222.7 6.9 %collective-permute-start.3 = (bf16[64,128]{1,0:T(8,128)(2,1)S(1)}, bf16[64,128]{1,0:T(8,128)(2,1)S(1)}, u32[]{:S(2)}, u32[]{:S(2)}) collective-permute-start(bf16[64,128]{1,0:T(8,128)(2,1)S(1)} %bitcast.153), channel_id=1, source_target_pairs={{0,2},{1,3},{2,0},{3,1},{4,6},{5,7},{6,4},{7,5},{8,10},{9,11},{10,... | collective-permute-start | bytes 49160 | tf_op jit(solution)/shard_map/ppermute | solution.py:88
  224.9 5.2 %collective-permute-start.4 = (bf16[64,128]{1,0:T(8,128)(2,1)S(1)}, bf16[64,128]{1,0:T(8,128)(2,1)S(1)}, u32[]{:S(2)}, u32[]{:S(2)}) collective-permute-start(bf16[64,128]{1,0:T(8,128)(2,1)S(1)} %bitcast.152), channel_id=1, source_target_pairs={{0,3},{1,2},{2,1},{3,0},{4,7},{5,6},{6,5},{7,4},{8,11},{9,10},{10,... | collective-permute-start | bytes 49160 | tf_op jit(solution)/shard_map/ppermute | solution.py:88
  225.3 7.0 %collective-permute-start.5 = (bf16[64,128]{1,0:T(8,128)(2,1)S(1)}, bf16[64,128]{1,0:T(8,128)(2,1)S(1)}, u32[]{:S(2)}, u32[]{:S(2)}) collective-permute-start(bf16[64,128]{1,0:T(8,128)(2,1)S(1)} %bitcast.151), channel_id=1, source_target_pairs={{0,4},{1,5},{2,6},{3,7},{4,0},{5,1},{6,2},{7,3},{8,12},{9,13},{10,... | collective-permute-start | bytes 49160 | tf_op jit(solution)/shard_map/ppermute | solution.py:88
  226.6 6.4 %collective-permute-start.6 = (bf16[64,128]{1,0:T(8,128)(2,1)S(1)}, bf16[64,128]{1,0:T(8,128)(2,1)S(1)}, u32[]{:S(2)}, u32[]{:S(2)}) collective-permute-start(bf16[64,128]{1,0:T(8,128)(2,1)S(1)} %bitcast.150), channel_id=1, source_target_pairs={{0,5},{1,4},{2,7},{3,6},{4,1},{5,0},{6,3},{7,2},{8,13},{9,12},{10,... | collective-permute-start | bytes 49160 | tf_op jit(solution)/shard_map/ppermute | solution.py:88
  227.5 8.5 %collective-permute-start.7 = (bf16[64,128]{1,0:T(8,128)(2,1)S(1)}, bf16[64,128]{1,0:T(8,128)(2,1)S(1)}, u32[]{:S(2)}, u32[]{:S(2)}) collective-permute-start(bf16[64,128]{1,0:T(8,128)(2,1)S(1)} %bitcast.149), channel_id=1, source_target_pairs={{0,6},{1,7},{2,4},{3,5},{4,2},{5,3},{6,0},{7,1},{8,14},{9,15},{10,... | collective-permute-start | bytes 49160 | tf_op jit(solution)/shard_map/ppermute | solution.py:88
  229.6 6.9 %collective-permute-start.8 = (bf16[64,128]{1,0:T(8,128)(2,1)S(1)}, bf16[64,128]{1,0:T(8,128)(2,1)S(1)}, u32[]{:S(2)}, u32[]{:S(2)}) collective-permute-start(bf16[64,128]{1,0:T(8,128)(2,1)S(1)} %bitcast.148), channel_id=1, source_target_pairs={{0,7},{1,6},{2,5},{3,4},{4,3},{5,2},{6,1},{7,0},{8,15},{9,14},{10,... | collective-permute-start | bytes 49160 | tf_op jit(solution)/shard_map/ppermute | solution.py:88
  230.1 9.0 %collective-permute-start.9 = (bf16[64,128]{1,0:T(8,128)(2,1)S(1)}, bf16[64,128]{1,0:T(8,128)(2,1)S(1)}, u32[]{:S(2)}, u32[]{:S(2)}) collective-permute-start(bf16[64,128]{1,0:T(8,128)(2,1)S(1)} %bitcast.147), channel_id=1, source_target_pairs={{0,8},{1,9},{2,10},{3,11},{4,12},{5,13},{6,14},{7,15},{8,0},{9,1},... | collective-permute-start | bytes 49160 | tf_op jit(solution)/shard_map/ppermute | solution.py:88
  232.3 8.0 %collective-permute-start.10 = (bf16[64,128]{1,0:T(8,128)(2,1)S(1)}, bf16[64,128]{1,0:T(8,128)(2,1)S(1)}, u32[]{:S(2)}, u32[]{:S(2)}) collective-permute-start(bf16[64,128]{1,0:T(8,128)(2,1)S(1)} %bitcast.146), channel_id=1, source_target_pairs={{0,9},{1,8},{2,11},{3,10},{4,13},{5,12},{6,15},{7,14},{8,1},{9,0},... | collective-permute-start | bytes 49160 | tf_op jit(solution)/shard_map/ppermute | solution.py:88
  233.0 9.9 %collective-permute-start.11 = (bf16[64,128]{1,0:T(8,128)(2,1)S(1)}, bf16[64,128]{1,0:T(8,128)(2,1)S(1)}, u32[]{:S(2)}, u32[]{:S(2)}) collective-permute-start(bf16[64,128]{1,0:T(8,128)(2,1)S(1)} %bitcast.145), channel_id=1, source_target_pairs={{0,10},{1,11},{2,8},{3,9},{4,14},{5,15},{6,12},{7,13},{8,2},{9,3},... | collective-permute-start | bytes 49160 | tf_op jit(solution)/shard_map/ppermute | solution.py:88
  236.0 8.6 %collective-permute-start.12 = (bf16[64,128]{1,0:T(8,128)(2,1)S(1)}, bf16[64,128]{1,0:T(8,128)(2,1)S(1)}, u32[]{:S(2)}, u32[]{:S(2)}) collective-permute-start(bf16[64,128]{1,0:T(8,128)(2,1)S(1)} %bitcast.144), channel_id=1, source_target_pairs={{0,11},{1,10},{2,9},{3,8},{4,15},{5,14},{6,13},{7,12},{8,3},{9,2},... | collective-permute-start | bytes 49160 | tf_op jit(solution)/shard_map/ppermute | solution.py:88
  236.5 8.0 %collective-permute-start.13 = (bf16[64,128]{1,0:T(8,128)(2,1)S(1)}, bf16[64,128]{1,0:T(8,128)(2,1)S(1)}, u32[]{:S(2)}, u32[]{:S(2)}) collective-permute-start(bf16[64,128]{1,0:T(8,128)(2,1)S(1)} %bitcast.143), channel_id=1, source_target_pairs={{0,12},{1,13},{2,14},{3,15},{4,8},{5,9},{6,10},{7,11},{8,4},{9,5},... | collective-permute-start | bytes 49160 | tf_op jit(solution)/shard_map/ppermute | solution.py:88
  239.1 5.5 %collective-permute-start.14 = (bf16[64,128]{1,0:T(8,128)(2,1)S(1)}, bf16[64,128]{1,0:T(8,128)(2,1)S(1)}, u32[]{:S(2)}, u32[]{:S(2)}) collective-permute-start(bf16[64,128]{1,0:T(8,128)(2,1)S(1)} %bitcast.142), channel_id=1, source_target_pairs={{0,13},{1,12},{2,15},{3,14},{4,9},{5,8},{6,11},{7,10},{8,5},{9,4},... | collective-permute-start | bytes 49160 | tf_op jit(solution)/shard_map/ppermute | solution.py:88
  240.3 5.4 %collective-permute-start.15 = (bf16[64,128]{1,0:T(8,128)(2,1)S(1)}, bf16[64,128]{1,0:T(8,128)(2,1)S(1)}, u32[]{:S(2)}, u32[]{:S(2)}) collective-permute-start(bf16[64,128]{1,0:T(8,128)(2,1)S(1)} %bitcast.141), channel_id=1, source_target_pairs={{0,14},{1,15},{2,12},{3,13},{4,10},{5,11},{6,8},{7,9},{8,6},{9,7},... | collective-permute-start | bytes 49160 | tf_op jit(solution)/shard_map/ppermute | solution.py:88
  242.9 6.3 %collective-permute-start.16 = (bf16[64,128]{1,0:T(8,128)(2,1)S(1)}, bf16[64,128]{1,0:T(8,128)(2,1)S(1)}, u32[]{:S(2)}, u32[]{:S(2)}) collective-permute-start(bf16[64,128]{1,0:T(8,128)(2,1)S(1)} %bitcast.140), channel_id=1, source_target_pairs={{0,15},{1,14},{2,13},{3,12},{4,11},{5,10},{6,9},{7,8},{8,7},{9,6},... | collective-permute-start | bytes 49160 | tf_op jit(solution)/shard_map/ppermute | solution.py:88
  244.6 12.2 %copy-start.3 = (s32[1,4]{1,0:T(1,128)S(1)}, s32[1,4]{1,0:T(1,128)}, u32[]{:S(2)}) copy-start(s32[1,4]{1,0:T(1,128)} %param.15) | copy-start | bytes 52
  250.0 104.8 %copy-start.2 = (s32[4]{0:T(128)S(1)}, s32[4]{0:T(128)}, u32[]{:S(2)}) copy-start(s32[4]{0:T(128)} %param.17) | copy-start | bytes 52
  250.6 9.5 %collective-permute-start.20 = (bf16[128,128]{1,0:T(8,128)(2,1)S(1)}, bf16[128,128]{1,0:T(8,128)(2,1)S(1)}, u32[]{:S(2)}, u32[]{:S(2)}) collective-permute-start(bf16[128,128]{1,0:T(8,128)(2,1)S(1)} %multiply_convert_fusion), channel_id=1, source_target_pairs={{4,0},{5,1},{6,2},{7,3},{8,4},{9,5},{10,6},{11,7},{12,8},{13,9},{1... | collective-permute-start | bytes 98312 | tf_op jit(solution)/shard_map/ppermute | solution.py:36
  251.9 8.5 %collective-permute-start.19 = (bf16[128,128]{1,0:T(8,128)(2,1)S(1)}, bf16[128,128]{1,0:T(8,128)(2,1)S(1)}, u32[]{:S(2)}, u32[]{:S(2)}) collective-permute-start(bf16[128,128]{1,0:T(8,128)(2,1)S(1)} %multiply_convert_fusion), channel_id=1, source_target_pairs={{3,0},{4,1},{5,2},{6,3},{7,4},{8,5},{9,6},{10,7},{11,8},{12,9},{13... | collective-permute-start | bytes 98312 | tf_op jit(solution)/shard_map/ppermute | solution.py:36
  253.2 7.2 %collective-permute-start.18 = (bf16[128,128]{1,0:T(8,128)(2,1)S(1)}, bf16[128,128]{1,0:T(8,128)(2,1)S(1)}, u32[]{:S(2)}, u32[]{:S(2)}) collective-permute-start(bf16[128,128]{1,0:T(8,128)(2,1)S(1)} %multiply_convert_fusion), channel_id=1, source_target_pairs={{2,0},{3,1},{4,2},{5,3},{6,4},{7,5},{8,6},{9,7},{10,8},{11,9},{12,... | collective-permute-start | bytes 98312 | tf_op jit(solution)/shard_map/ppermute | solution.py:36
  254.5 6.2 %collective-permute-start.17 = (bf16[128,128]{1,0:T(8,128)(2,1)S(1)}, bf16[128,128]{1,0:T(8,128)(2,1)S(1)}, u32[]{:S(2)}, u32[]{:S(2)}) collective-permute-start(bf16[128,128]{1,0:T(8,128)(2,1)S(1)} %multiply_convert_fusion), channel_id=1, source_target_pairs={{1,0},{2,1},{3,2},{4,3},{5,4},{6,5},{7,6},{8,7},{9,8},{10,9},{11,1... | collective-permute-start | bytes 98312 | tf_op jit(solution)/shard_map/ppermute | solution.py:36
Sparse Core Ops, SparseCore 0:
  261.5 93.3 all-reduce.1
